TPU v7x, 256 devices: a whole 4x4x8 slice. The times are simulated.
256 devices in a mesh: pairs: 32 (over x, y, core), tm: 8 (over z).
Axes of the slice: x: 4, y: 4, z: 8, core: 2. Of those that a mesh axis runs over, the one named last changes fastest.
Arguments:
- spectra: bfloat16 [2, 8, 1024, 4096], P(None, 'tm', 'pairs')
- pair_blocks: int32 [32, 4, 2], replicated, may hold values from 0 to 31, as said below
- block_count: int32 [32], replicated, may hold values from 1 to 4, as said below
Outputs:
- stacked: float32 [128, 128, 2048], P('pairs', None, 'tm')
Inputs may be any that keep to these rules, and one draw needn't show every extreme that they name: pair_blocks[p, k] names two different channel blocks; block j holds channels j * 128 to (j + 1) * 128 - 1. Owner p's pair blocks are its slots 0 to block_count[p] - 1; its later slots are empty and their rows of stacked are zero.
All inputs are finite; a program needn't handle non-finite values.
Results may differ from a plain program's by a relative error of at most 0.006.
Values may be sent and summed in bfloat16 or wider, within the bound.
No kernel may reach another device: no remote copies, remote signals or barrier semaphores. Data moves between devices by JAX's collectives and lax.ppermute only.
A program may use at most 128 MiB of HBM per device.

v0:
```python
import functools
import math

import jax
import jax.numpy as jnp
import ml_dtypes
import numpy as np
from jax import lax
from jax.experimental import pallas as pl
from jax.experimental.pallas import tpu as pltpu
from jax.sharding import PartitionSpec as P

C = 4096
CB = 128
NF = 1024
FIRST_BIN = 16
FFT_LEN = 8192
LAGS = 2048
SMOOTH = 32
MAXB = 4
HOURS = 8
OWNERS = 32
amp_floor = 0.2

CHIPS = OWNERS // 2
BINS = NF // OWNERS
CHIP_BINS = 2 * BINS
LAG_PART = LAGS // HOURS
RANK_CHIP = 28
RANK_PART = 48
ROWS_CHIP = 2 * RANK_CHIP
ROWS_PART = 2 * RANK_PART
STEP = 2.0 * math.pi / FFT_LEN


def slepian(points, half_width, count):
    n = np.arange(points, dtype=np.float64)
    tri = np.diag(((points - 1) / 2.0 - n) ** 2 * math.cos(2.0 * math.pi * half_width))
    off = n[1:] * (points - n[1:]) / 2.0
    tri = tri + np.diag(off, 1) + np.diag(off, -1)
    vectors = np.linalg.eigh(tri)[1][:, ::-1][:, :count]
    return vectors * np.where(vectors[points // 2] < 0, -1.0, 1.0)


def split_rounded(table):
    high = table.astype(ml_dtypes.bfloat16)
    low = (table - high.astype(np.float64)).astype(ml_dtypes.bfloat16)
    return high, low


def real_form(table):
    return np.block([[table.real, -table.imag], [table.imag, table.real]])


@functools.cache
def tables():
    chip_basis = slepian(CHIP_BINS, (LAGS / 2 + 4) / FFT_LEN, RANK_CHIP)
    part_basis = slepian(NF, (LAG_PART / 2 + 0.5) / FFT_LEN, RANK_PART)
    bins = np.arange(NF) - (NF - 1) / 2.0
    lags = np.arange(LAG_PART) - LAG_PART // 2
    mid_bin = FIRST_BIN + (NF - 1) / 2.0
    compress = np.kron(np.eye(2), chip_basis.T)
    parts = []
    for part in range(HOURS // 2):
        mid_lag = LAG_PART * part - (LAGS - LAG_PART) // 2
        turned = np.exp(1j * STEP * (bins + mid_bin) * mid_lag)[:, None] * part_basis
        turned = turned.reshape(CHIPS, CHIP_BINS, RANK_PART)
        blocks = [(chip_basis.T @ turned[chip]).T for chip in range(CHIPS)]
        parts.append(np.concatenate(blocks, axis=1))
    combine = np.concatenate([half for part in parts for half in (part.real, part.imag)], axis=0)
    waves = np.exp(1j * STEP * np.outer(lags, bins)) @ part_basis
    waves = waves * np.exp(1j * STEP * mid_bin * lags)[:, None] / math.sqrt(NF)
    expand = real_form(waves)
    row = np.arange(BINS)[:, None] + SMOOTH
    column = np.arange(BINS + 2 * SMOOTH)[None, :]
    window = (np.abs(row - column) <= SMOOTH).astype(ml_dtypes.bfloat16)
    turned = [window[:, -SMOOTH:], window[:, SMOOTH:-SMOOTH], window[:, :SMOOTH]]
    window = np.stack([window, np.concatenate(turned, axis=1)])
    halves = np.split(compress, 2 * CHIP_BINS // BINS, axis=1)
    by_core = []
    for core in range(2):
        own, twin = core, 1 - core
        ordered = [halves[own], halves[2 + own], halves[twin], halves[2 + twin]]
        by_core.append(np.concatenate(split_rounded(np.concatenate(ordered, axis=1)), axis=0))
    compress = np.stack(by_core)
    padded = np.zeros((2 * CB, 2 * LAG_PART), ml_dtypes.bfloat16)
    for index, half in enumerate(split_rounded(expand)):
        padded[index * CB : index * CB + ROWS_PART] = half.T
    expand = padded
    return window, compress, np.concatenate(split_rounded(combine), axis=0), expand


def magnitude_of(real, imag):
    real, imag = real.astype(jnp.float32), imag.astype(jnp.float32)
    return jnp.sqrt(real * real + imag * imag).astype(jnp.bfloat16)


def whiten(core, window, source, first, centre, second, white):
    chunk = 512
    weights = window[core]
    for start in range(0, C, chunk):
        lanes = slice(start, start + chunk)
        sizes = jnp.concatenate([first[:, lanes], centre[:, lanes], second[:, lanes]], axis=0)
        sums = jnp.dot(weights, sizes, preferred_element_type=jnp.float32)
        inverse = 1.0 / (sums * (1.0 / (2 * SMOOTH + 1)) + 1e-05)
        for part in range(2):
            value = source[part, :, lanes].astype(jnp.float32) * inverse
            white[part, :, lanes] = value.astype(jnp.bfloat16)


def cross_of(blocks, base, white):
    crossed = []
    for slot in range(MAXB):
        left = pl.ds(pl.multiple_of(blocks[base + 2 * slot] * CB, CB), CB)
        right = pl.ds(pl.multiple_of(blocks[base + 2 * slot + 1] * CB, CB), CB)
        left_re = white[0, :, left].astype(jnp.float32)
        left_im = white[1, :, left].astype(jnp.float32)
        right_re = white[0, :, right].astype(jnp.float32)
        right_im = white[1, :, right].astype(jnp.float32)
        real = left_re * right_re + left_im * right_im
        imag = left_im * right_re - left_re * right_im
        crossed.append(jnp.concatenate([real, imag], axis=0).astype(jnp.bfloat16))
    return jnp.concatenate(crossed, axis=1)


def own_kernel(blocks, most, count, window, own, near, own_size, twin_size, out, white):
    core = blocks[CHIPS * 2 * MAXB]
    whiten(core, window, own, near, own_size, twin_size, white)
    for chip in range(CHIPS):
        out[chip] = cross_of(blocks, chip * 2 * MAXB, white)


def twin_kernel(
    blocks, window, compress, twin, own_size, twin_size, far, own_cross, out, white
):
    core = blocks[CHIPS * 2 * MAXB]
    whiten(core, window, twin, own_size, twin_size, far, white)
    weights = compress[core]
    for chip in range(CHIPS):
        twin_cross = cross_of(blocks, chip * 2 * MAXB, white)
        cross = jnp.concatenate([own_cross[chip], twin_cross], axis=0)
        packed = jnp.dot(weights, cross, preferred_element_type=jnp.float32)
        out[chip] = (packed[:ROWS_CHIP] + packed[ROWS_CHIP:]).astype(jnp.bfloat16)


def combine_kernel(table, packed, out):
    wide = out.shape[2]
    real = [packed[chip, :RANK_CHIP, :wide] for chip in range(CHIPS)]
    imag = [packed[chip, RANK_CHIP:, :wide] for chip in range(CHIPS)]
    value = jnp.concatenate([jnp.concatenate(real, axis=0), jnp.concatenate(imag, axis=0)], axis=1)
    total = jnp.dot(table[...], value, preferred_element_type=jnp.float32)
    half = table.shape[0] // 2
    total = total[:half] + total[half:]
    for part in range(HOURS // 2):
        base = part * ROWS_PART
        real_rows = slice(base, base + RANK_PART)
        imag_rows = slice(base + RANK_PART, base + ROWS_PART)
        real_real, real_imag = total[real_rows, :wide], total[real_rows, wide:]
        imag_real, imag_imag = total[imag_rows, :wide], total[imag_rows, wide:]
        for where, sign in ((part, 1.0), (HOURS - 1 - part, -1.0)):
            both = [real_real - sign * imag_imag, real_imag + sign * imag_real]
            out[where] = jnp.concatenate(both, axis=0).astype(jnp.bfloat16)


def stack_kernel(live, expand, parts, out, result, sems):
    blank = jnp.zeros((CB - ROWS_PART, CB), jnp.bfloat16)
    copies = []
    for slot in range(MAXB):
        lanes = slice(slot * CB, (slot + 1) * CB)
        rows = []
        for hour in range(HOURS):
            part = jnp.concatenate([parts[hour, :, lanes], blank], axis=0).T
            rows.append(jnp.concatenate([part, part], axis=1))
        lagged = jnp.dot(
            jnp.concatenate(rows, axis=0), expand[...], preferred_element_type=jnp.float32
        )
        linear = mean_real = mean_imag = None
        for hour in range(HOURS):
            correlation = lagged[hour * CB : (hour + 1) * CB, :LAG_PART]
            quadrature = lagged[hour * CB : (hour + 1) * CB, LAG_PART:]
            power = correlation * correlation + quadrature * quadrature
            inverse = jnp.minimum(lax.rsqrt(power), 1.0 / amp_floor)
            unit_real = correlation * inverse
            unit_imag = quadrature * inverse
            if hour == 0:
                linear, mean_real, mean_imag = correlation, unit_real, unit_imag
            else:
                linear = linear + correlation
                mean_real = mean_real + unit_real
                mean_imag = mean_imag + unit_imag
        stacked = linear * (mean_real * mean_real + mean_imag * mean_imag) * (1.0 / HOURS**3)
        result[slot] = jnp.where(live[slot] > 0, stacked, jnp.zeros_like(stacked))
        copy = pltpu.make_async_copy(result.at[slot], out.at[slot], sems.at[slot])
        copy.start()
        copies.append(copy)
    for copy in copies:
        copy.wait()


def on_device(spectra, pair_blocks, block_count):
    owner = lax.axis_index("pairs")
    core = owner % 2
    window, compress, combine, expand = tables()
    spectra = spectra[:, 0]
    twins = [(i, i ^ 1) for i in range(OWNERS)]
    twin = lax.ppermute(spectra, "pairs", twins)
    own_size = magnitude_of(spectra[0], spectra[1])
    last = OWNERS - 1
    near_pairs = [(i, i + 1) for i in range(1, last, 2)] + [(i, i - 1) for i in range(2, last, 2)]
    near = lax.ppermute(own_size, "pairs", near_pairs)
    twin_size = magnitude_of(twin[0], twin[1])
    slots = lax.dynamic_index_in_dim(
        pair_blocks.reshape(CHIPS, 2, 2 * MAXB), core, 1, keepdims=False
    )
    slots = jnp.concatenate([slots.reshape(-1), core[None]])
    count = lax.dynamic_index_in_dim(block_count, owner, 0, keepdims=False)
    live = (lax.broadcasted_iota(jnp.int32, (MAXB, 1, 1), 0) < count).astype(jnp.float32)
    most = jnp.max(jnp.where(lax.iota(jnp.int32, OWNERS) % 2 == core, block_count, 0))
    first, last_live = jnp.int32(0), jnp.int32(MAXB - 1)
    branches = [lax.clamp(first, value - 1, last_live) for value in (most, count)]
    near, twin_size, slots, live, *branches = lax.optimization_barrier(
        (near, twin_size, slots, live, *branches)
    )
    far = lax.ppermute(near, "pairs", twins)
    vmem = pl.BlockSpec(memory_space=pltpu.VMEM)
    smem = pl.BlockSpec(memory_space=pltpu.SMEM)
    limit = pltpu.CompilerParams(vmem_limit_bytes=32 * 2**20)
    combine = lax.optimization_barrier(jnp.asarray(combine))
    white = pltpu.VMEM((2, BINS, C), jnp.bfloat16)
    own_cross = pl.pallas_call(
        own_kernel,
        out_shape=jax.ShapeDtypeStruct((CHIPS, 2 * BINS, MAXB * CB), jnp.bfloat16),
        in_specs=[smem] * 3 + [vmem] * 5,
        out_specs=vmem,
        scratch_shapes=[white],
        compiler_params=limit,
        name="own_cross",
    )(slots, *(branch[None] for branch in branches), window, spectra, near, own_size, twin_size)
    packed = pl.pallas_call(
        twin_kernel,
        out_shape=jax.ShapeDtypeStruct((CHIPS, ROWS_CHIP, MAXB * CB), jnp.bfloat16),
        in_specs=[smem] + [vmem] * 7,
        out_specs=vmem,
        scratch_shapes=[white],
        compiler_params=limit,
        name="twin_cross",
    )(slots, window, compress, twin, own_size, twin_size, far, own_cross)
    groups = [list(range(0, OWNERS, 2)), list(range(1, OWNERS, 2))]

    def widen(parts, slots):
        return jnp.pad(parts, ((0, 0), (0, 0), (0, (MAXB - slots) * CB)))

    def between_chips(slots):
        def exchange(packed):
            packed = lax.all_to_all(
                packed[:, :, : slots * CB], "pairs", 0, 0, axis_index_groups=groups, tiled=True
            )
            return widen(packed, slots)

        return exchange

    packed = lax.switch(most - 1, [between_chips(slots) for slots in range(1, MAXB + 1)], packed)

    def with_live(live):
        def exchange(packed, combine):
            parts = pl.pallas_call(
                combine_kernel,
                out_shape=jax.ShapeDtypeStruct((HOURS, ROWS_PART, live * CB), jnp.bfloat16),
                in_specs=[vmem] * 2,
                out_specs=vmem,
                compiler_params=limit,
                name=f"combine_{live}",
            )(combine, packed)
            parts = lax.all_to_all(parts, "tm", 0, 0, tiled=True)
            return widen(parts, live)

        return exchange

    parts = lax.switch(
        count - 1, [with_live(live) for live in range(1, MAXB + 1)], packed, combine
    )
    return pl.pallas_call(
        stack_kernel,
        out_shape=jax.ShapeDtypeStruct((MAXB, CB, LAG_PART), jnp.float32),
        in_specs=[vmem] * 3,
        out_specs=pl.BlockSpec(memory_space=pl.ANY),
        scratch_shapes=[
            pltpu.VMEM((MAXB, CB, LAG_PART), jnp.float32),
            pltpu.SemaphoreType.DMA((MAXB,)),
        ],
        compiler_params=limit,
        name="stack",
    )(live, expand, parts)


def solution(mesh):
    return jax.shard_map(
        on_device,
        mesh=mesh,
        in_specs=(P(None, "tm", "pairs", None), P(), P()),
        out_specs=P("pairs", None, "tm"),
        check_vma=False,
    )
```

profile of v0, /device:TPU:4, one launch (start us, length us, event | category | flops | bytes accessed | tf_op | source)
XLA Modules:
  0.0 65.0 jit_solution(14308569116085313375)
XLA Ops:
  0.0 1.2 %fusion.own_size = bf16[32,4096]{1,0:T(8,128)(2,1)S(1)} fusion(bf16[2,1,32,4096]{3,2,1,0:T(8,128)(2,1)} %param.15), kind=kLoop, calls=%fused_computation.2 | loop fusion | flops 786432 | bytes 786432 | tf_op jit(solution)/shard_map/sqrt | solution.py:95
  1.3 5.0 %collective-permute-start = (bf16[32,4096]{1,0:T(8,128)(2,1)S(1)}, bf16[32,4096]{1,0:T(8,128)(2,1)S(1)}, u32[]{:S(2)}, u32[]{:S(2)}) collective-permute-start(bf16[32,4096]{1,0:T(8,128)(2,1)S(1)} %fusion.own_size), channel_id=1, source_target_pairs={{8,16},{24,32},{40,48},{56,64},{72,80},{88,96},{104,112},{120,128}... | collective-permute-start | bytes 786440 | tf_op jit(solution)/shard_map/ppermute | solution.py:210
  6.3 0.6 copy-done.6
  6.9 0.6 dynamic_slice.9
  7.5 0.7 %fusion.2 = s32[]{:T(128)} fusion(s32[32]{0:T(128)S(1)} %copy-done.6, s32[]{:T(128)} %select_n.25), kind=kLoop, calls=%fused_computation.8 | loop fusion | flops 287 | bytes 136 | tf_op jit(solution)/shard_map/reduce_max | solution.py:218
  9.5 0.0 copy-done.5
  9.5 0.1 reshape.37
  9.6 0.1 constant_dynamic-slice_fusion
  9.7 0.2 copy.9
  9.9 0.1 reshape.38
  10.0 0.7 %compare_convert_fusion.live = f32[4,1,1]{2,1,0:T(1,128)S(1)} fusion(s32[]{:T(128)} %bitcast.4), kind=kLoop, calls=%fused_computation.4 | loop fusion | flops 8 | bytes 20 | tf_op jit(solution)/shard_map/convert_element_type | solution.py:217
  10.7 0.0 copy-start.2
  10.7 0.2 fusion.1.twin_size
  10.9 0.2 collective-permute-done.near
  11.1 0.3 copy-done.2
  11.4 1.4 %own_cross.1 = bf16[16,64,512]{2,1,0:T(8,128)(2,1)S(1)} custom-call(s32[129]{0:T(256)S(1)} %pad_add_fusion.blocks, s32[1]{0:T(128)} %bitcast.5.most, s32[1]{0:T(128)} %bitcast.6.count, bf16[2,32,96]{2,1,0:T(8,128)(2,1)S(1)} %copy-done.2, bf16[2,32,4096]{2,1,0:T(8,128)(2,1)S(1)} %bitcast.14, bf16[32,4096]{1,0:T(8,128)(2,1)S(1)} %collective-permute-done.near, ...), custom_call_target="tpu_custom_call" | custom-call | tf_op jit(solution)/shard_map/own_cross/pallas_call | solution.py:230
  12.8 1.9 %twin_cross.1 = bf16[16,56,512]{2,1,0:T(8,128)(2,1)S(1)} custom-call(s32[129]{0:T(256)S(1)} %pad_add_fusion.blocks, bf16[2,32,96]{2,1,0:T(8,128)(2,1)S(1)} %copy-done.2, bf16[2,112,128]{2,1,0:T(8,128)(2,1)S(1)} %copy-done.3, bf16[2,32,4096]{2,1,0:T(8,128)(2,1)S(1)} %collective-permute-done.1.twin, bf16[32,4096]{1,0:T(8,128)(2,1)S(1)} %fusion.own_size, ...), custom_call_target="tpu_custom_call" | custom-call | tf_op jit(solution)/shard_map/twin_cross/pallas_call | solution.py:239
  14.8 0.0 copy-start.4
  14.8 20.9 %conditional.2 = (bf16[16,56,512]{2,1,0:T(8,128)(2,1)S(1)}) conditional(s32[]{:T(128)} %clamp.8, bf16[16,56,512]{2,1,0:T(8,128)(2,1)S(1)} %twin_cross.1, bf16[16,56,512]{2,1,0:T(8,128)(2,1)S(1)} %twin_cross.1, bf16[16,56,512]{2,1,0:T(8,128)(2,1)S(1)} %twin_cross.1, bf16[16,56,512]{2,1,0:T(8,128)(2,1)S(1)} %twin_cross.1), branch_computations={%region_1.2_spmd, %region_2.3_spmd, %region_3.4_spmd, %region_4.5_... | conditional | bytes 4358154 | solution.py:262
  14.8 20.9 %all_to_all.35 = bf16[16,56,512]{2,1,0:T(8,128)(2,1)S(1)} all-to-all(bf16[16,56,512]{2,1,0:T(8,128)(2,1)S(1)} %param.3), channel_id=1, replica_groups={{0,16,32,48,64,80,96,112,128,144,160,176,192,208,224,240},{8,24,40,56,7..., dimensions={0} | all-to-all | bytes 1835008 | tf_op jit(solution)/shard_map/cond/branch_3_fun/all_to_all | solution.py:255
  35.7 26.8 %conditional.3 = (bf16[8,96,512]{2,1,0:T(8,128)(2,1)S(1)}) conditional(s32[]{:T(128)} %clamp.9, (bf16[768,448]{1,0:T(8,128)(2,1)S(1)}, bf16[16,56,512]{2,1,0:T(8,128)(2,1)S(1)}) %tuple.40, (bf16[768,448]{1,0:T(8,128)(2,1)S(1)}, bf16[16,56,512]{2,1,0:T(8,128)(2,1)S(1)}) %tuple.41, (bf16[768,448]{1,0:T(8,128)(2,1)S(1)}, ...), branch_computations={%region_5.6_spmd, %region_6.7_spmd, %region_7.8_spmd, %region_8.9_... | conditional | bytes 2555914 | solution.py:279
  35.7 1.0 %combine_4.1 = bf16[8,96,512]{2,1,0:T(8,128)(2,1)S(1)} custom-call(bf16[768,448]{1,0:T(8,128)(2,1)S(1)} %get-tuple-element.41.table, bf16[16,56,512]{2,1,0:T(8,128)(2,1)S(1)} %get-tuple-element.42.packed), custom_call_target="tpu_custom_call" | custom-call | tf_op jit(solution)/shard_map/cond/branch_3_fun/combine_4/pallas_call | solution.py:266
  36.7 25.8 %all_to_all.39 = bf16[8,96,512]{2,1,0:T(8,128)(2,1)S(1)} all-to-all(bf16[8,96,512]{2,1,0:T(8,128)(2,1)S(1)} %combine_4.1), channel_id=1, replica_groups=mesh['pairs'=32,'tm'=8] {'tm'}, dimensions={0} | all-to-all | bytes 1572864 | tf_op jit(solution)/shard_map/cond/branch_3_fun/all_to_all | solution.py:274
  62.5 2.5 %stack.1 = f32[4,128,256]{2,1,0:T(8,128)} custom-call(f32[4,1,1]{2,1,0:T(1,128)S(1)} %compare_convert_fusion.live, bf16[256,512]{1,0:T(8,128)(2,1)S(1)} %copy-done.1, bf16[8,96,512]{2,1,0:T(8,128)(2,1)S(1)} %get-tuple-element.56.parts), custom_call_target="tpu_custom_call" | custom-call | tf_op jit(solution)/shard_map/stack/pallas_call | solution.py:282
  (14 shorter events, 0.0 us)
Async XLA Ops:
  0.0 10.7 %collective-permute-start.1 = (bf16[2,32,4096]{2,1,0:T(8,128)(2,1)}, bf16[2,32,4096]{2,1,0:T(8,128)(2,1)S(1)}, u32[]{:S(2)}, u32[]{:S(2)}) collective-permute-start(bf16[2,32,4096]{2,1,0:T(8,128)(2,1)} %bitcast.13), channel_id=1, source_target_pairs={{0,8},{8,0},{16,24},{24,16},{32,40},{40,32},{48,56},{56,48},{64,72... | collective-permute-start | bytes 1572872 | tf_op jit(solution)/shard_map/ppermute | solution.py:206
  1.3 9.8 %collective-permute-start = (bf16[32,4096]{1,0:T(8,128)(2,1)S(1)}, bf16[32,4096]{1,0:T(8,128)(2,1)S(1)}, u32[]{:S(2)}, u32[]{:S(2)}) collective-permute-start(bf16[32,4096]{1,0:T(8,128)(2,1)S(1)} %fusion.own_size), channel_id=1, source_target_pairs={{8,16},{24,32},{40,48},{56,64},{72,80},{88,96},{104,112},{120,128}... | collective-permute-start | bytes 786440 | tf_op jit(solution)/shard_map/ppermute | solution.py:210
  6.3 0.7 %copy-start.6 = (s32[32]{0:T(128)S(1)}, s32[32]{0:T(128)}, u32[]{:S(2)}) copy-start(s32[32]{0:T(128)} %param.17) | copy-start | bytes 388
  8.8 0.7 %copy-start.5 = (s32[32,4,2]{0,2,1:T(2,128)S(1)}, s32[32,4,2]{0,2,1:T(2,128)}, u32[]{:S(2)}) copy-start(s32[32,4,2]{0,2,1:T(2,128)} %param.16) | copy-start | bytes 3076
  9.5 1.5 %copy-start = (bf16[2,1,32,4096]{3,2,1,0:T(8,128)(2,1)S(1)}, bf16[2,1,32,4096]{3,2,1,0:T(8,128)(2,1)}, u32[]{:S(2)}) copy-start(bf16[2,1,32,4096]{3,2,1,0:T(8,128)(2,1)} %param.15) | copy-start | bytes 1572868
  10.7 0.7 %copy-start.2 = (bf16[2,32,96]{2,1,0:T(8,128)(2,1)S(1)}, bf16[2,32,96]{2,1,0:T(8,128)(2,1)}, u32[]{:S(2)}) copy-start(bf16[2,32,96]{2,1,0:T(8,128)(2,1)} %constant.75.clone.window) | copy-start | bytes 36868
  11.1 1.8 %collective-permute-start.2 = (bf16[32,4096]{1,0:T(8,128)(2,1)S(1)}, bf16[32,4096]{1,0:T(8,128)(2,1)S(1)}, u32[]{:S(2)}, u32[]{:S(2)}) collective-permute-start(bf16[32,4096]{1,0:T(8,128)(2,1)S(1)} %collective-permute-done.near), channel_id=1, source_target_pairs={{0,8},{8,0},{16,24},{24,16},{32,40},{40,32},{48,56},{56,48},{64,72... | collective-permute-start | bytes 786440 | tf_op jit(solution)/shard_map/ppermute | solution.py:224
  11.4 1.5 %copy-start.3 = (bf16[2,112,128]{2,1,0:T(8,128)(2,1)S(1)}, bf16[2,112,128]{2,1,0:T(8,128)(2,1)}, u32[]{:S(2)}) copy-start(bf16[2,112,128]{2,1,0:T(8,128)(2,1)} %constant.76.clone.compress) | copy-start | bytes 172036
  14.8 21.0 %copy-start.4 = (bf16[768,448]{1,0:T(8,128)(2,1)S(1)}, bf16[768,448]{1,0:T(8,128)(2,1)}, u32[]{:S(2)}) copy-start(bf16[768,448]{1,0:T(8,128)(2,1)} %constant.74.clone) | copy-start | bytes 2064388
  35.7 26.8 %copy-start.1 = (bf16[256,512]{1,0:T(8,128)(2,1)S(1)}, bf16[256,512]{1,0:T(8,128)(2,1)}, u32[]{:S(2)}) copy-start(bf16[256,512]{1,0:T(8,128)(2,1)} %constant.77.clone.expand) | copy-start | bytes 786436
where the time goes:
time: 65.6 us; the launch traced here: 65 us
  blocking collectives  46.7 us (71%)
  Pallas kernels  6.82 us (10%)
  starting transfers between devices  5.01 us (8%)
  other arithmetic  2.79 us (4%)
  local copies, waits for them, and re-layouts  2.03 us (3%)
  between operations  1.45 us (2%)
    all_to_all x1, blocking collectives, exchange(): parts = lax.all_to_all(parts, 'tm', 0, 0, tiled=True)  25.8 us
    all_to_all x1, blocking collectives, exchange(): lax.all_to_all(packed[:, :, :slots * CB], 'pairs', 0, 0, axis_index_group...  20.9 us
    ppermute x1, starting transfers between devices, on_device(): near = lax.ppermute(own_size, 'pairs', near_pairs)  5.01 us
    pallas_call x1, Pallas kernels, on_device(): pl.pallas_call(stack_kernel, out_shape=jax.ShapeDtypeStruct((MAXB, CB, LA...  2.49 us
    pallas_call x1, Pallas kernels, on_device(): pl.pallas_call(twin_kernel, out_shape=jax.ShapeDtypeStruct((CHIPS, ROWS_C...  1.92 us
    sqrt x2, other arithmetic, magnitude_of(): return jnp.sqrt(real * real + imag * imag).astype(jnp.bfloat16)  1.46 us
    pallas_call x1, Pallas kernels, on_device(): pl.pallas_call(own_kernel, out_shape=jax.ShapeDtypeStruct((CHIPS, 2 * BIN...  1.43 us
  transfers between devices with their start and end apart: 3, of which 1 were waited for; matrix products, arithmetic and copies ran while one was open for 6% of the time, Pallas kernels for 2%

commit v1 on v0

--- a/solution.py
+++ b/solution.py
@@ -71,11 +71,6 @@
     waves = np.exp(1j * STEP * np.outer(lags, bins)) @ part_basis
     waves = waves * np.exp(1j * STEP * mid_bin * lags)[:, None] / math.sqrt(NF)
     expand = real_form(waves)
-    row = np.arange(BINS)[:, None] + SMOOTH
-    column = np.arange(BINS + 2 * SMOOTH)[None, :]
-    window = (np.abs(row - column) <= SMOOTH).astype(ml_dtypes.bfloat16)
-    turned = [window[:, -SMOOTH:], window[:, SMOOTH:-SMOOTH], window[:, :SMOOTH]]
-    window = np.stack([window, np.concatenate(turned, axis=1)])
     halves = np.split(compress, 2 * CHIP_BINS // BINS, axis=1)
     by_core = []
     for core in range(2):
@@ -87,7 +82,7 @@
     for index, half in enumerate(split_rounded(expand)):
         padded[index * CB : index * CB + ROWS_PART] = half.T
     expand = padded
-    return window, compress, np.concatenate(split_rounded(combine), axis=0), expand
+    return compress, np.concatenate(split_rounded(combine), axis=0), expand
 
 
 def magnitude_of(real, imag):
@@ -95,9 +90,20 @@
     return jnp.sqrt(real * real + imag * imag).astype(jnp.bfloat16)
 
 
-def whiten(core, window, source, first, centre, second, white):
+def window_weights(core):
+    shape = (BINS, 3 * BINS)
+    row = lax.broadcasted_iota(jnp.int32, shape, 0)
+    column = lax.broadcasted_iota(jnp.int32, shape, 1)
+    place = column % BINS
+    below = jnp.where(core == 0, BINS - 1 - column, column - 2 * BINS) >= 0
+    ahead = jnp.where(below, place - row, row - place)
+    centre = (column >= BINS) & (column < 2 * BINS)
+    return jnp.where(centre | (ahead >= 0), 1.0, 0.0).astype(jnp.bfloat16)
+
+
+def whiten(core, source, first, centre, second, white):
     chunk = 512
-    weights = window[core]
+    weights = window_weights(core)
     for start in range(0, C, chunk):
         lanes = slice(start, start + chunk)
         sizes = jnp.concatenate([first[:, lanes], centre[:, lanes], second[:, lanes]], axis=0)
@@ -123,18 +129,18 @@
     return jnp.concatenate(crossed, axis=1)
 
 
-def own_kernel(blocks, most, count, window, own, near, own_size, twin_size, out, white):
+def own_kernel(blocks, most, count, own, near, own_size, twin_size, out, white):
     core = blocks[CHIPS * 2 * MAXB]
-    whiten(core, window, own, near, own_size, twin_size, white)
+    whiten(core, own, near, own_size, twin_size, white)
     for chip in range(CHIPS):
         out[chip] = cross_of(blocks, chip * 2 * MAXB, white)
 
 
 def twin_kernel(
-    blocks, window, compress, twin, own_size, twin_size, far, own_cross, out, white
+    blocks, compress, twin, own_size, twin_size, far, own_cross, out, white
 ):
     core = blocks[CHIPS * 2 * MAXB]
-    whiten(core, window, twin, own_size, twin_size, far, white)
+    whiten(core, twin, own_size, twin_size, far, white)
     weights = compress[core]
     for chip in range(CHIPS):
         twin_cross = cross_of(blocks, chip * 2 * MAXB, white)
@@ -200,7 +206,7 @@
 def on_device(spectra, pair_blocks, block_count):
     owner = lax.axis_index("pairs")
     core = owner % 2
-    window, compress, combine, expand = tables()
+    compress, combine, expand = tables()
     spectra = spectra[:, 0]
     twins = [(i, i ^ 1) for i in range(OWNERS)]
     twin = lax.ppermute(spectra, "pairs", twins)
@@ -230,21 +236,21 @@
     own_cross = pl.pallas_call(
         own_kernel,
         out_shape=jax.ShapeDtypeStruct((CHIPS, 2 * BINS, MAXB * CB), jnp.bfloat16),
-        in_specs=[smem] * 3 + [vmem] * 5,
+        in_specs=[smem] * 3 + [vmem] * 4,
         out_specs=vmem,
         scratch_shapes=[white],
         compiler_params=limit,
         name="own_cross",
-    )(slots, *(branch[None] for branch in branches), window, spectra, near, own_size, twin_size)
+    )(slots, *(branch[None] for branch in branches), spectra, near, own_size, twin_size)
     packed = pl.pallas_call(
         twin_kernel,
         out_shape=jax.ShapeDtypeStruct((CHIPS, ROWS_CHIP, MAXB * CB), jnp.bfloat16),
-        in_specs=[smem] + [vmem] * 7,
+        in_specs=[smem] + [vmem] * 6,
         out_specs=vmem,
         scratch_shapes=[white],
         compiler_params=limit,
         name="twin_cross",
-    )(slots, window, compress, twin, own_size, twin_size, far, own_cross)
+    )(slots, compress, twin, own_size, twin_size, far, own_cross)
     groups = [list(range(0, OWNERS, 2)), list(range(1, OWNERS, 2))]
 
     def widen(parts, slots):

time: 65.6 us -> 64.2 us (0.979)
  the two profiles are of different devices: /device:TPU:4 before, /device:TPU:8 now
where the time goes in v1:
time: 64.2 us; the launch traced here: 64.9 us
  blocking collectives  47.8 us (74%)
  Pallas kernels  6.82 us (11%)
  starting transfers between devices  4.3 us (7%)
  other arithmetic  2.76 us (4%)
  local copies, waits for them, and re-layouts  1.71 us (3%)
  between operations  1.39 us (2%)
    all_to_all x1, blocking collectives, exchange(): parts = lax.all_to_all(parts, 'tm', 0, 0, tiled=True)  25.2 us
    all_to_all x1, blocking collectives, exchange(): lax.all_to_all(packed[:, :, :slots * CB], 'pairs', 0, 0, axis_index_group...  22.6 us
    ppermute x1, starting transfers between devices, on_device(): near = lax.ppermute(own_size, 'pairs', near_pairs)  4.21 us
    pallas_call x1, Pallas kernels, on_device(): pl.pallas_call(stack_kernel, out_shape=jax.ShapeDtypeStruct((MAXB, CB, LA...  2.49 us
    pallas_call x1, Pallas kernels, on_device(): pl.pallas_call(twin_kernel, out_shape=jax.ShapeDtypeStruct((CHIPS, ROWS_C...  1.91 us
    sqrt x2, other arithmetic, magnitude_of(): return jnp.sqrt(real * real + imag * imag).astype(jnp.bfloat16)  1.46 us
    pallas_call x1, Pallas kernels, on_device(): pl.pallas_call(own_kernel, out_shape=jax.ShapeDtypeStruct((CHIPS, 2 * BIN...  1.43 us
  transfers between devices with their start and end apart: 3, of which 1 were waited for; matrix products, arithmetic and copies ran while one was open for 6% of the time, Pallas kernels for 2%

profile of v1, /device:TPU:8, one launch (start us, length us, event | category | flops | bytes accessed | tf_op | source)
XLA Modules:
  0.0 64.9 jit_solution(12291520461442385088)
XLA Ops:
  0.0 1.2 %fusion.own_size = bf16[32,4096]{1,0:T(8,128)(2,1)S(1)} fusion(bf16[2,1,32,4096]{3,2,1,0:T(8,128)(2,1)} %param.14), kind=kLoop, calls=%fused_computation.2 | loop fusion | flops 786432 | bytes 786432 | tf_op jit(solution)/shard_map/sqrt | solution.py:90
  1.3 4.2 %collective-permute-start = (bf16[32,4096]{1,0:T(8,128)(2,1)S(1)}, bf16[32,4096]{1,0:T(8,128)(2,1)S(1)}, u32[]{:S(2)}, u32[]{:S(2)}) collective-permute-start(bf16[32,4096]{1,0:T(8,128)(2,1)S(1)} %fusion.own_size), channel_id=1, source_target_pairs={{8,16},{24,32},{40,48},{56,64},{72,80},{88,96},{104,112},{120,128}... | collective-permute-start | bytes 786440 | tf_op jit(solution)/shard_map/ppermute | solution.py:216
  5.5 0.6 copy-done.5
  6.1 0.6 dynamic_slice.9
  6.7 0.6 fusion.2
  8.6 0.0 copy-done.4
  8.6 0.1 reshape.37
  8.7 0.1 constant_dynamic-slice_fusion
  8.8 0.2 copy.8
  9.0 0.1 reshape.38
  9.1 0.7 %compare_convert_fusion.live = f32[4,1,1]{2,1,0:T(1,128)S(1)} fusion(s32[]{:T(128)} %bitcast.4), kind=kLoop, calls=%fused_computation.4 | loop fusion | flops 8 | bytes 20 | tf_op jit(solution)/shard_map/convert_element_type | solution.py:223
  9.8 0.2 fusion.1.twin_size
  10.0 0.1 collective-permute-start.2
  10.1 0.0 copy-start.2
  10.1 1.4 %own_cross.1 = bf16[16,64,512]{2,1,0:T(8,128)(2,1)S(1)} custom-call(s32[129]{0:T(256)S(1)} %pad_add_fusion.blocks, s32[1]{0:T(128)} %bitcast.5.most, s32[1]{0:T(128)} %bitcast.6.count, bf16[2,32,4096]{2,1,0:T(8,128)(2,1)S(1)} %bitcast.14, bf16[32,4096]{1,0:T(8,128)(2,1)S(1)} %collective-permute-done.near, bf16[32,4096]{1,0:T(8,128)(2,1)S(1)} %fusion.own_size, ...), custom_call_target="tpu_custom_call" | custom-call | tf_op jit(solution)/shard_map/own_cross/pallas_call | solution.py:236
  11.6 0.1 collective-permute-done.2.far
  11.6 1.9 %twin_cross.1 = bf16[16,56,512]{2,1,0:T(8,128)(2,1)S(1)} custom-call(s32[129]{0:T(256)S(1)} %pad_add_fusion.blocks, bf16[2,112,128]{2,1,0:T(8,128)(2,1)S(1)} %copy-done.2, bf16[2,32,4096]{2,1,0:T(8,128)(2,1)S(1)} %collective-permute-done.1.twin, bf16[32,4096]{1,0:T(8,128)(2,1)S(1)} %fusion.own_size, bf16[32,4096]{1,0:T(8,128)(2,1)S(1)} %fusion.1.twin_size, ...), custom_call_target="tpu_custom_call" | custom-call | tf_op jit(solution)/shard_map/twin_cross/pallas_call | solution.py:245
  13.5 0.0 copy-start.3
  13.6 22.6 %conditional.2 = (bf16[16,56,512]{2,1,0:T(8,128)(2,1)S(1)}) conditional(s32[]{:T(128)} %clamp.8, bf16[16,56,512]{2,1,0:T(8,128)(2,1)S(1)} %twin_cross.1, bf16[16,56,512]{2,1,0:T(8,128)(2,1)S(1)} %twin_cross.1, bf16[16,56,512]{2,1,0:T(8,128)(2,1)S(1)} %twin_cross.1, bf16[16,56,512]{2,1,0:T(8,128)(2,1)S(1)} %twin_cross.1), branch_computations={%region_1.2_spmd, %region_2.3_spmd, %region_3.4_spmd, %region_4.5_... | conditional | bytes 4358154 | solution.py:268
  13.6 22.6 %all_to_all.35 = bf16[16,56,512]{2,1,0:T(8,128)(2,1)S(1)} all-to-all(bf16[16,56,512]{2,1,0:T(8,128)(2,1)S(1)} %param.3), channel_id=1, replica_groups={{0,16,32,48,64,80,96,112,128,144,160,176,192,208,224,240},{8,24,40,56,7..., dimensions={0} | all-to-all | bytes 1835008 | tf_op jit(solution)/shard_map/cond/branch_3_fun/all_to_all | solution.py:261
  36.2 26.2 %conditional.3 = (bf16[8,96,512]{2,1,0:T(8,128)(2,1)S(1)}) conditional(s32[]{:T(128)} %clamp.9, (bf16[768,448]{1,0:T(8,128)(2,1)S(1)}, bf16[16,56,512]{2,1,0:T(8,128)(2,1)S(1)}) %tuple.40, (bf16[768,448]{1,0:T(8,128)(2,1)S(1)}, bf16[16,56,512]{2,1,0:T(8,128)(2,1)S(1)}) %tuple.41, (bf16[768,448]{1,0:T(8,128)(2,1)S(1)}, ...), branch_computations={%region_5.6_spmd, %region_6.7_spmd, %region_7.8_spmd, %region_8.9_... | conditional | bytes 2555914 | solution.py:285
  36.2 1.0 %combine_4.1 = bf16[8,96,512]{2,1,0:T(8,128)(2,1)S(1)} custom-call(bf16[768,448]{1,0:T(8,128)(2,1)S(1)} %get-tuple-element.41.table, bf16[16,56,512]{2,1,0:T(8,128)(2,1)S(1)} %get-tuple-element.42.packed), custom_call_target="tpu_custom_call" | custom-call | tf_op jit(solution)/shard_map/cond/branch_3_fun/combine_4/pallas_call | solution.py:272
  37.2 25.2 %all_to_all.39 = bf16[8,96,512]{2,1,0:T(8,128)(2,1)S(1)} all-to-all(bf16[8,96,512]{2,1,0:T(8,128)(2,1)S(1)} %combine_4.1), channel_id=1, replica_groups=mesh['pairs'=32,'tm'=8] {'tm'}, dimensions={0} | all-to-all | bytes 1572864 | tf_op jit(solution)/shard_map/cond/branch_3_fun/all_to_all | solution.py:280
  62.4 2.5 %stack.1 = f32[4,128,256]{2,1,0:T(8,128)} custom-call(f32[4,1,1]{2,1,0:T(1,128)S(1)} %compare_convert_fusion.live, bf16[256,512]{1,0:T(8,128)(2,1)S(1)} %copy-done.1, bf16[8,96,512]{2,1,0:T(8,128)(2,1)S(1)} %get-tuple-element.56.parts), custom_call_target="tpu_custom_call" | custom-call | tf_op jit(solution)/shard_map/stack/pallas_call | solution.py:288
  (12 shorter events, 0.0 us)
Async XLA Ops:
  0.0 9.8 %collective-permute-start.1 = (bf16[2,32,4096]{2,1,0:T(8,128)(2,1)}, bf16[2,32,4096]{2,1,0:T(8,128)(2,1)S(1)}, u32[]{:S(2)}, u32[]{:S(2)}) collective-permute-start(bf16[2,32,4096]{2,1,0:T(8,128)(2,1)} %bitcast.13), channel_id=1, source_target_pairs={{0,8},{8,0},{16,24},{24,16},{32,40},{40,32},{48,56},{56,48},{64,72... | collective-permute-start | bytes 1572872 | tf_op jit(solution)/shard_map/ppermute | solution.py:212
  1.3 8.7 %collective-permute-start = (bf16[32,4096]{1,0:T(8,128)(2,1)S(1)}, bf16[32,4096]{1,0:T(8,128)(2,1)S(1)}, u32[]{:S(2)}, u32[]{:S(2)}) collective-permute-start(bf16[32,4096]{1,0:T(8,128)(2,1)S(1)} %fusion.own_size), channel_id=1, source_target_pairs={{8,16},{24,32},{40,48},{56,64},{72,80},{88,96},{104,112},{120,128}... | collective-permute-start | bytes 786440 | tf_op jit(solution)/shard_map/ppermute | solution.py:216
  5.5 0.7 %copy-start.5 = (s32[32]{0:T(128)S(1)}, s32[32]{0:T(128)}, u32[]{:S(2)}) copy-start(s32[32]{0:T(128)} %param.16) | copy-start | bytes 388
  7.9 0.7 %copy-start.4 = (s32[32,4,2]{0,2,1:T(2,128)S(1)}, s32[32,4,2]{0,2,1:T(2,128)}, u32[]{:S(2)}) copy-start(s32[32,4,2]{0,2,1:T(2,128)} %param.15) | copy-start | bytes 3076
  8.6 1.5 %copy-start = (bf16[2,1,32,4096]{3,2,1,0:T(8,128)(2,1)S(1)}, bf16[2,1,32,4096]{3,2,1,0:T(8,128)(2,1)}, u32[]{:S(2)}) copy-start(bf16[2,1,32,4096]{3,2,1,0:T(8,128)(2,1)} %param.14) | copy-start | bytes 1572868
  10.0 1.6 %collective-permute-start.2 = (bf16[32,4096]{1,0:T(8,128)(2,1)S(1)}, bf16[32,4096]{1,0:T(8,128)(2,1)S(1)}, u32[]{:S(2)}, u32[]{:S(2)}) collective-permute-start(bf16[32,4096]{1,0:T(8,128)(2,1)S(1)} %collective-permute-done.near), channel_id=1, source_target_pairs={{0,8},{8,0},{16,24},{24,16},{32,40},{40,32},{48,56},{56,48},{64,72... | collective-permute-start | bytes 786440 | tf_op jit(solution)/shard_map/ppermute | solution.py:230
  10.1 1.5 %copy-start.2 = (bf16[2,112,128]{2,1,0:T(8,128)(2,1)S(1)}, bf16[2,112,128]{2,1,0:T(8,128)(2,1)}, u32[]{:S(2)}) copy-start(bf16[2,112,128]{2,1,0:T(8,128)(2,1)} %constant.73.clone.compress) | copy-start | bytes 172036
  13.5 22.6 %copy-start.3 = (bf16[768,448]{1,0:T(8,128)(2,1)S(1)}, bf16[768,448]{1,0:T(8,128)(2,1)}, u32[]{:S(2)}) copy-start(bf16[768,448]{1,0:T(8,128)(2,1)} %constant.72.clone) | copy-start | bytes 2064388
  36.2 26.2 %copy-start.1 = (bf16[256,512]{1,0:T(8,128)(2,1)S(1)}, bf16[256,512]{1,0:T(8,128)(2,1)}, u32[]{:S(2)}) copy-start(bf16[256,512]{1,0:T(8,128)(2,1)} %constant.74.clone.expand) | copy-start | bytes 786436

commit v2 on v0

--- a/solution.py
+++ b/solution.py
@@ -96,7 +96,7 @@
 
 
 def whiten(core, window, source, first, centre, second, white):
-    chunk = 512
+    chunk = 2048
     weights = window[core]
     for start in range(0, C, chunk):
         lanes = slice(start, start + chunk)

time: 65.6 us -> 65.6 us (level)
  the two profiles are of different devices: /device:TPU:4 before, /device:TPU:20 now
where the time goes in v2:
time: 65.6 us; the launch traced here: 66.2 us
  blocking collectives  49.9 us (76%)
  Pallas kernels  6.61 us (10%)
  starting transfers between devices  2.98 us (5%)
  other arithmetic  2.79 us (4%)
  local copies, waits for them, and re-layouts  1.78 us (3%)
  between operations  1.46 us (2%)
    all_to_all x1, blocking collectives, exchange(): parts = lax.all_to_all(parts, 'tm', 0, 0, tiled=True)  28.6 us
    all_to_all x1, blocking collectives, exchange(): lax.all_to_all(packed[:, :, :slots * CB], 'pairs', 0, 0, axis_index_group...  21.3 us
    pallas_call x1, Pallas kernels, on_device(): pl.pallas_call(stack_kernel, out_shape=jax.ShapeDtypeStruct((MAXB, CB, LA...  2.48 us
    ppermute x1, starting transfers between devices, on_device(): near = lax.ppermute(own_size, 'pairs', near_pairs)  2.47 us
    pallas_call x1, Pallas kernels, on_device(): pl.pallas_call(twin_kernel, out_shape=jax.ShapeDtypeStruct((CHIPS, ROWS_C...  1.92 us
    sqrt x2, other arithmetic, magnitude_of(): return jnp.sqrt(real * real + imag * imag).astype(jnp.bfloat16)  1.46 us
    pallas_call x1, Pallas kernels, on_device(): pl.pallas_call(own_kernel, out_shape=jax.ShapeDtypeStruct((CHIPS, 2 * BIN...  1.43 us
  transfers between devices with their start and end apart: 3, of which 1 were waited for; matrix products, arithmetic and copies ran while one was open for 6% of the time, Pallas kernels for 2%

profile of v2, /device:TPU:20, one launch (start us, length us, event | category | flops | bytes accessed | tf_op | source)
XLA Modules:
  0.0 66.2 jit_solution(14308569116085313375)
XLA Ops:
  0.0 1.2 %fusion.own_size = bf16[32,4096]{1,0:T(8,128)(2,1)S(1)} fusion(bf16[2,1,32,4096]{3,2,1,0:T(8,128)(2,1)} %param.15), kind=kLoop, calls=%fused_computation.2 | loop fusion | flops 786432 | bytes 786432 | tf_op jit(solution)/shard_map/sqrt | solution.py:95
  1.3 2.5 %collective-permute-start = (bf16[32,4096]{1,0:T(8,128)(2,1)S(1)}, bf16[32,4096]{1,0:T(8,128)(2,1)S(1)}, u32[]{:S(2)}, u32[]{:S(2)}) collective-permute-start(bf16[32,4096]{1,0:T(8,128)(2,1)S(1)} %fusion.own_size), channel_id=1, source_target_pairs={{8,16},{24,32},{40,48},{56,64},{72,80},{88,96},{104,112},{120,128}... | collective-permute-start | bytes 786440 | tf_op jit(solution)/shard_map/ppermute | solution.py:210
  3.8 0.6 copy-done.6
  4.4 0.6 dynamic_slice.9
  5.0 0.7 %fusion.2 = s32[]{:T(128)} fusion(s32[32]{0:T(128)S(1)} %copy-done.6, s32[]{:T(128)} %select_n.25), kind=kLoop, calls=%fused_computation.8 | loop fusion | flops 287 | bytes 136 | tf_op jit(solution)/shard_map/reduce_max | solution.py:218
  7.0 0.0 copy-done.5
  7.0 0.1 reshape.37
  7.1 0.1 constant_dynamic-slice_fusion
  7.2 0.2 copy.9
  7.3 0.1 reshape.38
  7.5 0.7 compare_convert_fusion.live
  8.1 0.0 copy-start.2
  8.1 0.2 fusion.1.twin_size
  8.4 0.6 collective-permute-done.near
  8.9 0.5 collective-permute-start.2
  9.5 1.4 %own_cross.1 = bf16[16,64,512]{2,1,0:T(8,128)(2,1)S(1)} custom-call(s32[129]{0:T(256)S(1)} %pad_add_fusion.blocks, s32[1]{0:T(128)} %bitcast.5.most, s32[1]{0:T(128)} %bitcast.6.count, bf16[2,32,96]{2,1,0:T(8,128)(2,1)S(1)} %copy-done.2, bf16[2,32,4096]{2,1,0:T(8,128)(2,1)S(1)} %bitcast.14, bf16[32,4096]{1,0:T(8,128)(2,1)S(1)} %collective-permute-done.near, ...), custom_call_target="tpu_custom_call" | custom-call | tf_op jit(solution)/shard_map/own_cross/pallas_call | solution.py:230
  10.9 1.9 %twin_cross.1 = bf16[16,56,512]{2,1,0:T(8,128)(2,1)S(1)} custom-call(s32[129]{0:T(256)S(1)} %pad_add_fusion.blocks, bf16[2,32,96]{2,1,0:T(8,128)(2,1)S(1)} %copy-done.2, bf16[2,112,128]{2,1,0:T(8,128)(2,1)S(1)} %copy-done.3, bf16[2,32,4096]{2,1,0:T(8,128)(2,1)S(1)} %collective-permute-done.1.twin, bf16[32,4096]{1,0:T(8,128)(2,1)S(1)} %fusion.own_size, ...), custom_call_target="tpu_custom_call" | custom-call | tf_op jit(solution)/shard_map/twin_cross/pallas_call | solution.py:239
  12.9 21.3 %conditional.2 = (bf16[16,56,512]{2,1,0:T(8,128)(2,1)S(1)}) conditional(s32[]{:T(128)} %clamp.8, bf16[16,56,512]{2,1,0:T(8,128)(2,1)S(1)} %twin_cross.1, bf16[16,56,512]{2,1,0:T(8,128)(2,1)S(1)} %twin_cross.1, bf16[16,56,512]{2,1,0:T(8,128)(2,1)S(1)} %twin_cross.1, bf16[16,56,512]{2,1,0:T(8,128)(2,1)S(1)} %twin_cross.1), branch_computations={%region_1.2_spmd, %region_2.3_spmd, %region_3.4_spmd, %region_4.5_... | conditional | bytes 4358154 | solution.py:262
  12.9 21.3 %all_to_all.35 = bf16[16,56,512]{2,1,0:T(8,128)(2,1)S(1)} all-to-all(bf16[16,56,512]{2,1,0:T(8,128)(2,1)S(1)} %param.3), channel_id=1, replica_groups={{0,16,32,48,64,80,96,112,128,144,160,176,192,208,224,240},{8,24,40,56,7..., dimensions={0} | all-to-all | bytes 1835008 | tf_op jit(solution)/shard_map/cond/branch_3_fun/all_to_all | solution.py:255
  34.2 29.5 %conditional.3 = (bf16[8,96,512]{2,1,0:T(8,128)(2,1)S(1)}) conditional(s32[]{:T(128)} %clamp.9, (bf16[768,448]{1,0:T(8,128)(2,1)S(1)}, bf16[16,56,512]{2,1,0:T(8,128)(2,1)S(1)}) %tuple.40, (bf16[768,448]{1,0:T(8,128)(2,1)S(1)}, bf16[16,56,512]{2,1,0:T(8,128)(2,1)S(1)}) %tuple.41, (bf16[768,448]{1,0:T(8,128)(2,1)S(1)}, ...), branch_computations={%region_5.6_spmd, %region_6.7_spmd, %region_7.8_spmd, %region_8.9_... | conditional | bytes 2555914 | solution.py:279
  34.2 0.8 %combine_3.1 = bf16[8,96,384]{2,1,0:T(8,128)(2,1)S(1)} custom-call(bf16[768,448]{1,0:T(8,128)(2,1)S(1)} %get-tuple-element.39.table, bf16[16,56,512]{2,1,0:T(8,128)(2,1)S(1)} %get-tuple-element.40.packed), custom_call_target="tpu_custom_call" | custom-call | tf_op jit(solution)/shard_map/cond/branch_2_fun/combine_3/pallas_call | solution.py:266
  35.0 28.6 %all_to_all.38 = bf16[8,96,384]{2,1,0:T(8,128)(2,1)S(1)} all-to-all(bf16[8,96,384]{2,1,0:T(8,128)(2,1)S(1)} %combine_3.1), channel_id=1, replica_groups=mesh['pairs'=32,'tm'=8] {'tm'}, dimensions={0} | all-to-all | bytes 1179648 | tf_op jit(solution)/shard_map/cond/branch_2_fun/all_to_all | solution.py:274
  63.6 0.1 pad.23
  63.7 2.5 %stack.1 = f32[4,128,256]{2,1,0:T(8,128)} custom-call(f32[4,1,1]{2,1,0:T(1,128)S(1)} %compare_convert_fusion.live, bf16[256,512]{1,0:T(8,128)(2,1)S(1)} %copy-done.1, bf16[8,96,512]{2,1,0:T(8,128)(2,1)S(1)} %get-tuple-element.56.parts), custom_call_target="tpu_custom_call" | custom-call | tf_op jit(solution)/shard_map/stack/pallas_call | solution.py:282
  (15 shorter events, 0.0 us)
Async XLA Ops:
  0.0 8.1 %collective-permute-start.1 = (bf16[2,32,4096]{2,1,0:T(8,128)(2,1)}, bf16[2,32,4096]{2,1,0:T(8,128)(2,1)S(1)}, u32[]{:S(2)}, u32[]{:S(2)}) collective-permute-start(bf16[2,32,4096]{2,1,0:T(8,128)(2,1)} %bitcast.13), channel_id=1, source_target_pairs={{0,8},{8,0},{16,24},{24,16},{32,40},{40,32},{48,56},{56,48},{64,72... | collective-permute-start | bytes 1572872 | tf_op jit(solution)/shard_map/ppermute | solution.py:206
  1.3 7.7 %collective-permute-start = (bf16[32,4096]{1,0:T(8,128)(2,1)S(1)}, bf16[32,4096]{1,0:T(8,128)(2,1)S(1)}, u32[]{:S(2)}, u32[]{:S(2)}) collective-permute-start(bf16[32,4096]{1,0:T(8,128)(2,1)S(1)} %fusion.own_size), channel_id=1, source_target_pairs={{8,16},{24,32},{40,48},{56,64},{72,80},{88,96},{104,112},{120,128}... | collective-permute-start | bytes 786440 | tf_op jit(solution)/shard_map/ppermute | solution.py:210
  3.7 0.7 copy-start.6
  6.3 0.7 %copy-start.5 = (s32[32,4,2]{0,2,1:T(2,128)S(1)}, s32[32,4,2]{0,2,1:T(2,128)}, u32[]{:S(2)}) copy-start(s32[32,4,2]{0,2,1:T(2,128)} %param.16) | copy-start | bytes 3076
  7.0 2.5 %copy-start = (bf16[2,1,32,4096]{3,2,1,0:T(8,128)(2,1)S(1)}, bf16[2,1,32,4096]{3,2,1,0:T(8,128)(2,1)}, u32[]{:S(2)}) copy-start(bf16[2,1,32,4096]{3,2,1,0:T(8,128)(2,1)} %param.15) | copy-start | bytes 1572868
  8.1 1.3 %copy-start.2 = (bf16[2,32,96]{2,1,0:T(8,128)(2,1)S(1)}, bf16[2,32,96]{2,1,0:T(8,128)(2,1)}, u32[]{:S(2)}) copy-start(bf16[2,32,96]{2,1,0:T(8,128)(2,1)} %constant.75.clone.window) | copy-start | bytes 36868
  8.9 2.0 %collective-permute-start.2 = (bf16[32,4096]{1,0:T(8,128)(2,1)S(1)}, bf16[32,4096]{1,0:T(8,128)(2,1)S(1)}, u32[]{:S(2)}, u32[]{:S(2)}) collective-permute-start(bf16[32,4096]{1,0:T(8,128)(2,1)S(1)} %collective-permute-done.near), channel_id=1, source_target_pairs={{0,8},{8,0},{16,24},{24,16},{32,40},{40,32},{48,56},{56,48},{64,72... | collective-permute-start | bytes 786440 | tf_op jit(solution)/shard_map/ppermute | solution.py:224
  9.5 1.4 %copy-start.3 = (bf16[2,112,128]{2,1,0:T(8,128)(2,1)S(1)}, bf16[2,112,128]{2,1,0:T(8,128)(2,1)}, u32[]{:S(2)}) copy-start(bf16[2,112,128]{2,1,0:T(8,128)(2,1)} %constant.76.clone.compress) | copy-start | bytes 172036
  12.8 21.3 %copy-start.4 = (bf16[768,448]{1,0:T(8,128)(2,1)S(1)}, bf16[768,448]{1,0:T(8,128)(2,1)}, u32[]{:S(2)}) copy-start(bf16[768,448]{1,0:T(8,128)(2,1)} %constant.74.clone) | copy-start | bytes 2064388
  34.2 29.5 %copy-start.1 = (bf16[256,512]{1,0:T(8,128)(2,1)S(1)}, bf16[256,512]{1,0:T(8,128)(2,1)}, u32[]{:S(2)}) copy-start(bf16[256,512]{1,0:T(8,128)(2,1)} %constant.77.clone.expand) | copy-start | bytes 786436
